TPU v7x, 32 devices: a whole 2x2x4 slice. The times are simulated.
32 devices in a mesh: grp: 2 (over y), gx: 4 (over z), gy: 2 (over x), gz: 2 (over core).
Axes of the slice: x: 2, y: 2, z: 4, core: 2. Of those that a mesh axis runs over, the one named last changes fastest.
Arguments:
- hidden_in: bfloat16 [64, 18432], P(('grp', 'gy', 'gz'), 'gx'), parts along dimension 0
- ln_gain: float32 [18432], P('gx'), may hold values from 0.1 to 1.9
- w_query: bfloat16 [18432, 12288], P('gx', ('gy', 'gz')), may hold values from -0.046875 to 0.046875
- w_keyval: bfloat16 [18432, 512], P('gx', ('gy', 'gz')), may hold values from -0.046875 to 0.046875
- w_output: bfloat16 [12288, 18432], P(('gy', 'gz'), 'gx'), may hold values from -0.3125 to 0.3125
- key_cache: bfloat16 [64, 512, 256], P(('grp', 'gx', 'gy', 'gz')), parts along dimension 0, as said below
- value_cache: bfloat16 [64, 512, 256], P(('grp', 'gx', 'gy', 'gz')), parts along dimension 0, may hold values from -6 to 6
- lengths: int32 [64], P(('grp', 'gx', 'gy', 'gz')), parts along dimension 0, may hold values from 1 to 512, as said below
- positions: int32 [64], P(('grp', 'gx', 'gy', 'gz')), parts along dimension 0, may hold values from 0 to 8191
Outputs:
- attn_out: float32 [64, 18432], P(('grp', 'gy', 'gz'), 'gx'), parts along dimension 0
There are 2 independent parts, one for each index of `grp`. A program takes and returns all parts, laid end to end along the dimension named above; an argument that names none is the same for every part. Nothing has to cross between parts.
Inputs may be any that keep to these rules, and one draw needn't show every extreme that they name: Each sequence attends to its first lengths cache slots and its new token; in every draw some sequence uses all 512 slots. `key_cache`: keys already carry their rotary positions.
All inputs are finite; a program needn't handle non-finite values.
Results may differ from a plain program's by a relative error of at most 0.012.
The roundings to bfloat16 on the way count: a program that leaves them out, or rounds other values in their place, can miss the bound.
Values may be sent and summed in bfloat16 or wider, within the bound.
A program may use at most 128 MiB of HBM per device.

v0:
```python
import jax
import jax.numpy as jnp
from jax import lax
from jax.sharding import PartitionSpec as P

D = 18432
DH = 256


def rotary(values, places):
    half = values.shape[-1] // 2
    freqs = jnp.exp(-jnp.log(10000.0) * jnp.arange(half, dtype=jnp.float32) / half)
    angles = places.astype(jnp.float32)[:, None] * freqs[None, :]
    while angles.ndim < values.ndim:
        angles = angles[:, None, :]
    cosine = jnp.cos(angles)
    sine = jnp.sin(angles)
    first = values[..., :half]
    second = values[..., half:]
    return jnp.concatenate([first * cosine - second * sine, second * cosine + first * sine], -1)


def attend(query2d, keyval2d, key_cache, value_cache, lengths, positions):
    count = query2d.shape[0]
    heads_here = query2d.shape[1] // DH
    query = query2d.reshape(count, heads_here, DH).astype(jnp.float32)
    rot_query = rotary(query, positions).astype(jnp.bfloat16)
    rot_key = rotary(keyval2d[:, :DH].astype(jnp.float32), positions).astype(jnp.bfloat16)
    new_value = keyval2d[:, DH:]
    scale = DH ** (-0.5)
    scores = (
        jnp.einsum("bhd,bld->bhl", rot_query, key_cache, preferred_element_type=jnp.float32) * scale
    )
    selfish = (
        jnp.einsum("bhd,bd->bh", rot_query, rot_key, preferred_element_type=jnp.float32) * scale
    )
    live = jnp.arange(key_cache.shape[1], dtype=jnp.int32)[None, :] < lengths[:, None]
    live = live[:, None, :]
    masked = jnp.where(live, scores, -1e30)
    peak = jnp.maximum(jnp.max(masked, -1), selfish)
    expo = jnp.where(live, jnp.exp(masked - peak[..., None]), 0.0)
    expo_self = jnp.exp(selfish - peak)
    total = jnp.sum(expo, -1) + expo_self
    probs = (expo / total[..., None]).astype(jnp.bfloat16)
    probs_self = (expo_self / total).astype(jnp.bfloat16)
    mixed = jnp.einsum("bhl,bld->bhd", probs, value_cache, preferred_element_type=jnp.float32)
    mixed = (
        mixed
        + probs_self.astype(jnp.float32)[..., None] * new_value.astype(jnp.float32)[:, None, :]
    )
    return mixed.reshape(count, heads_here * DH).astype(jnp.bfloat16)


def per_device(
    hidden_in, ln_gain, w_query, w_keyval, w_output, key_cache, value_cache, lengths, positions
):
    xf = hidden_in.astype(jnp.float32)
    totals, squares = lax.psum((jnp.sum(xf, 1), jnp.sum(xf * xf, 1)), "gx")
    mean = totals / D
    var = squares / D - mean * mean
    centered = xf - mean[:, None]
    normed = (centered * lax.rsqrt(var + 1e-05)[:, None] * ln_gain[None, :]).astype(jnp.bfloat16)
    all_rows = lax.all_gather(normed, ("gy", "gz"), axis=0, tiled=True)
    query_cols = w_query.shape[1]
    first = jnp.dot(all_rows, w_query, preferred_element_type=jnp.float32)
    second = jnp.dot(all_rows, w_keyval, preferred_element_type=jnp.float32)
    projected = lax.psum_scatter(
        jnp.concatenate([first, second], 1), "gx", scatter_dimension=0, tiled=True
    ).astype(jnp.bfloat16)
    query_part = projected[:, :query_cols]
    keyval_part = projected[:, query_cols:]
    query_seq, keyval_seq = (
        lax.all_to_all(query_part, ("gy", "gz"), split_axis=0, concat_axis=1, tiled=True),
        lax.all_to_all(keyval_part, ("gy", "gz"), split_axis=0, concat_axis=1, tiled=True),
    )
    attended = attend(query_seq, keyval_seq, key_cache, value_cache, lengths, positions)
    head_block = lax.all_to_all(attended, ("gy", "gz"), split_axis=1, concat_axis=0, tiled=True)
    partials = jnp.dot(
        lax.all_gather(head_block, "gx", axis=0, tiled=True),
        w_output,
        preferred_element_type=jnp.float32,
    )
    return lax.psum_scatter(
        partials.astype(jnp.bfloat16), ("gy", "gz"), scatter_dimension=0, tiled=True
    ).astype(jnp.float32)


def solution(mesh):
    in_specs = (
        P(("grp", "gy", "gz"), "gx"),
        P("gx"),
        P("gx", ("gy", "gz")),
        P("gx", ("gy", "gz")),
        P(("gy", "gz"), "gx"),
        P(("grp", "gx", "gy", "gz"), None, None),
        P(("grp", "gx", "gy", "gz"), None, None),
        P(("grp", "gx", "gy", "gz")),
        P(("grp", "gx", "gy", "gz")),
    )
    out_specs = P(("grp", "gy", "gz"), "gx")
    return jax.shard_map(
        per_device, mesh=mesh, in_specs=in_specs, out_specs=out_specs, check_vma=False
    )
```

profile of v0, /device:TPU:0, one launch (start us, length us, event | category | flops | bytes accessed | tf_op | source)
XLA Modules:
  0.0 140.9 jit_solution(9452019721534691215)
XLA Ops:
  6.5 0.0 copy-start
  6.5 0.0 copy-start.5
  6.5 0.0 copy-start.2
  6.5 0.0 copy-start.4
  6.5 0.0 copy-start.1
  6.5 0.0 copy-start.3
  6.6 1.2 convert_reduce_fusion
  7.8 13.5 %all-reduce.1 = (f32[8]{0:T(128)S(1)}, f32[8]{0:T(128)S(1)}) all-reduce(f32[8]{0:T(128)S(1)} %get-tuple-element.6, f32[8]{0:T(128)S(1)} %get-tuple-element.5), channel_id=1, replica_groups=mesh['grp'=2,'gx'=4,'gy'=2,'gz'=2] {'gx'}, use_global_device_ids=true, to_apply=%region_3.0 | all-reduce | flops 16 | bytes 128 | tf_op jit(solution)/shard_map/psum | solution.py:58
  21.3 1.0 fusion.5
  22.2 5.9 %all_gather.6 = bf16[32,4608]{1,0:T(8,128)(2,1)S(1)} all-gather(bf16[8,4608]{1,0:T(8,128)(2,1)S(1)} %fusion.5), channel_id=1, replica_groups=mesh['grp'=2,'gx'=4,'gy'=2,'gz'=2] {'gy','gz'}, dimensions={0}, use_global_device_ids=true | all-gather | bytes 368640 | tf_op jit(solution)/shard_map/all_gather | solution.py:63
  28.2 11.5 %fusion.19 = f32[32,3072]{1,0:T(8,128)S(1)} fusion(bf16[32,4608]{1,0:T(8,128)(2,1)S(1)} %all_gather.6, bf16[4608,3072]{1,0:T(8,128)(2,1)} %param.11), kind=kOutput, calls=%fused_computation.47 | convolution fusion | flops 905969664 | bytes 28999680 | tf_op jit(solution)/shard_map/dot_general | solution.py:65
  39.7 0.0 copy-done
  39.7 0.3 fusion.20
  40.1 24.8 %all-reduce.3 = bf16[32,3200]{1,0:T(8,128)(2,1)S(1)} all-reduce(f32[32,3200]{1,0:T(8,128)S(1)} %pad_maximum_fusion), channel_id=2, replica_groups=mesh['grp'=2,'gx'=4,'gy'=2,'gz'=2] {'gx'}, use_global_device_ids=true, to_apply=%region_4.0.clone | all-reduce | flops 102400 | bytes 614400
  64.9 0.0 copy-done.5
  64.9 0.6 dynamic-slice
  66.2 0.6 slice.35
  66.8 3.2 %all-to-all-start.1 = ((bf16[4,2,128]{2,1,0:T(2,128)(2,1)}), bf16[4,2,128]{2,1,0:T(2,128)(2,1)S(1)}, u32[]{:S(2)}, u32[]{:S(2)}) async-start(bf16[4,2,128]{2,1,0:T(2,128)(2,1)} %bitcast.1), calls=%async_computation.1 | async-start | bytes 4096 | tf_op jit(solution)/shard_map/all_to_all | solution.py:74
  69.9 0.0 copy-done.2
  69.9 0.1 iota_compare_fusion
  70.0 0.0 copy-done.4
  70.0 0.6 all_to_all.36
  70.7 2.9 %all-to-all-done.1 = bf16[4,2,128]{2,1,0:T(2,128)(2,1)S(1)} async-done(((bf16[4,2,128]{2,1,0:T(2,128)(2,1)}), bf16[4,2,128]{2,1,0:T(2,128)(2,1)S(1)}, u32[]{:S(2)}, u32[]{:S(2)}) %all-to-all-start.1) | async-done | bytes 2080 | tf_op jit(solution)/shard_map/all_to_all | solution.py:74
  73.6 3.3 %all-to-all-start = ((bf16[4,2,3072]{2,1,0:T(2,128)(2,1)}), bf16[4,2,3072]{2,1,0:T(2,128)(2,1)S(1)}, u32[]{:S(2)}, u32[]{:S(2)}) async-start(bf16[4,2,3072]{2,1,0:T(2,128)(2,1)} %all_to_all.36), calls=%async_computation | async-start | bytes 98304 | tf_op jit(solution)/shard_map/all_to_all | solution.py:73
  76.9 0.0 reduce-scatter.2.cloned.1.call-start
  77.0 0.1 subtract_convert_fusion.1
  77.1 3.8 %all-to-all-done = bf16[4,2,3072]{2,1,0:T(2,128)(2,1)S(1)} async-done(((bf16[4,2,3072]{2,1,0:T(2,128)(2,1)}), bf16[4,2,3072]{2,1,0:T(2,128)(2,1)S(1)}, u32[]{:S(2)}, u32[]{:S(2)}) %all-to-all-start) | async-done | bytes 49184 | tf_op jit(solution)/shard_map/all_to_all | solution.py:73
  81.0 0.1 reshape.92
  81.1 0.1 fusion.11
  81.2 0.0 copy-done.1
  81.2 0.4 fusion.18
  81.6 0.2 fusion.2
  81.8 0.0 copy-done.3
  81.8 0.3 fusion.1
  82.1 6.4 %all_to_all.48 = bf16[2,4,3072]{2,0,1:T(2,128)(2,1)S(1)} all-to-all(bf16[2,4,3072]{2,0,1:T(2,128)(2,1)S(1)} %copy.16), channel_id=1, replica_groups=mesh['grp'=2,'gx'=4,'gy'=2,'gz'=2] {'gy','gz'}, dimensions={1} | all-to-all | bytes 98304 | tf_op jit(solution)/shard_map/all_to_all | solution.py:77
  88.6 13.9 %all_gather.7 = bf16[32,3072]{1,0:T(8,128)(2,1)S(1)} all-gather(bf16[8,3072]{1,0:T(8,128)(2,1)S(1)} %all_to_all.44), channel_id=1, replica_groups=mesh['grp'=2,'gx'=4,'gy'=2,'gz'=2] {'gx'}, dimensions={0}, use_global_device_ids=true | all-gather | bytes 245760 | tf_op jit(solution)/shard_map/all_gather | solution.py:79
  102.5 12.3 %convolution_convert_fusion = bf16[32,4608]{1,0:T(8,128)(2,1)} fusion(bf16[32,3072]{1,0:T(8,128)(2,1)S(1)} %all_gather.7, bf16[3072,4608]{1,0:T(8,128)(2,1)} %param.13), kind=kOutput, calls=%fused_computation | convolution fusion | flops 906117120 | bytes 28803072 | tf_op jit(solution)/shard_map/dot_general | solution.py:78
  114.8 0.0 reduce-scatter.2.cloned.1.call-update
  114.8 17.8 %reduce-scatter.2.cloned.1.call-done = bf16[8,4608]{1,0:T(8,128)(2,1)} async-done(((bf16[32,4608]{1,0:T(8,128)(2,1)}), bf16[8,4608]{1,0:T(8,128)(2,1)}) %reduce-scatter.2.cloned.1.call-update) | async-done | bytes 73744 | tf_op jit(solution)/shard_map/reduce_scatter | solution.py:83
  132.5 1.6 %convert_element_type.67 = f32[8,4608]{1,0:T(8,128)} convert(bf16[8,4608]{1,0:T(8,128)(2,1)} %reduce-scatter.2.cloned.1.call-done) | non-fusion elementwise | flops 36864 | bytes 221184 | tf_op jit(solution)/shard_map/convert_element_type | solution.py:85
  (16 shorter events, 0.3 us)
Async XLA Ops:
  6.5 33.2 %copy-start = (bf16[4608,128]{1,0:T(8,128)(2,1)S(1)}, bf16[4608,128]{1,0:T(8,128)(2,1)}, u32[]{:S(2)}) copy-start(bf16[4608,128]{1,0:T(8,128)(2,1)} %param.12) | copy-start | bytes 3538948
  6.5 58.4 %copy-start.5 = (u32[32]{0:T(128)S(1)}, u32[32]{0:T(128)}, u32[]{:S(2)}) copy-start(u32[32]{0:T(128)} %constant.26) | copy-start | bytes 388
  6.5 63.4 %copy-start.2 = (s32[2]{0:T(128)S(1)}, s32[2]{0:T(128)}, u32[]{:S(2)}) copy-start(s32[2]{0:T(128)} %param.16) | copy-start | bytes 28
  6.5 63.5 %copy-start.4 = (s32[2]{0:T(128)S(1)}, s32[2]{0:T(128)}, u32[]{:S(2)}) copy-start(s32[2]{0:T(128)} %param.17) | copy-start | bytes 28
  6.5 74.7 %copy-start.1 = (bf16[2,512,256]{2,1,0:T(8,128)(2,1)S(1)}, bf16[2,512,256]{2,1,0:T(8,128)(2,1)}, u32[]{:S(2)}) copy-start(bf16[2,512,256]{2,1,0:T(8,128)(2,1)} %param.14) | copy-start | bytes 1572868
  6.5 75.2 %copy-start.3 = (bf16[2,512,256]{2,1,0:T(8,128)(2,1)S(1)}, bf16[2,512,256]{2,1,0:T(8,128)(2,1)}, u32[]{:S(2)}) copy-start(bf16[2,512,256]{2,1,0:T(8,128)(2,1)} %param.15) | copy-start | bytes 1572868
  66.8 6.9 %all-to-all-start.1 = ((bf16[4,2,128]{2,1,0:T(2,128)(2,1)}), bf16[4,2,128]{2,1,0:T(2,128)(2,1)S(1)}, u32[]{:S(2)}, u32[]{:S(2)}) async-start(bf16[4,2,128]{2,1,0:T(2,128)(2,1)} %bitcast.1), calls=%async_computation.1 | async-start | bytes 4096 | tf_op jit(solution)/shard_map/all_to_all | solution.py:74
  73.6 7.3 %all-to-all-start = ((bf16[4,2,3072]{2,1,0:T(2,128)(2,1)}), bf16[4,2,3072]{2,1,0:T(2,128)(2,1)S(1)}, u32[]{:S(2)}, u32[]{:S(2)}) async-start(bf16[4,2,3072]{2,1,0:T(2,128)(2,1)} %all_to_all.36), calls=%async_computation | async-start | bytes 98304 | tf_op jit(solution)/shard_map/all_to_all | solution.py:73
  76.9 55.6 %reduce-scatter.2.cloned.1.call-start = ((), (), s32[]{:S(2)}) async-start(), calls=%async_computation.4 | async-start | bytes 368640 | tf_op jit(solution)/shard_map/reduce_scatter | solution.py:83
Sparse Core Ops, SparseCore 0:
  114.9 17.6 reduce-scatter.1
where the time goes:
time: 141 us
  blocking collectives  64.5 us (46%)
  matrix products  24.9 us (18%)
  waiting for transfers between devices  24.5 us (17%)
  between operations  14.3 us (10%)
  starting transfers between devices  6.48 us (5%)
  other arithmetic  4.27 us (3%)
  local copies, waits for them, and re-layouts  2.03 us (1%)
    unnamed x1, blocking collectives  24.8 us
    reduce_scatter x1, waiting for transfers between devices, per_device(): lax.psum_scatter(partials.astype(jnp.bfloat16), ('gy', 'gz'), scatter_dim...  17.8 us
    all_gather x1, blocking collectives, per_device(): lax.all_gather(head_block, 'gx', axis=0, tiled=True)  13.9 us
    psum x1, blocking collectives, per_device(): totals, squares = lax.psum((jnp.sum(xf, 1), jnp.sum(xf * xf, 1)), 'gx')  13.5 us
    dot_general x1, matrix products, per_device(): jnp.dot(lax.all_gather(head_block, 'gx', axis=0, tiled=True), w_output, p...  12.3 us
    dot_general x1, matrix products, per_device(): first = jnp.dot(all_rows, w_query, preferred_element_type=jnp.float32)  11.5 us
    all_to_all x1, blocking collectives, per_device(): lax.all_to_all(attended, ('gy', 'gz'), split_axis=1, concat_axis=0, tiled...  6.39 us
    all_gather x1, blocking collectives, per_device(): all_rows = lax.all_gather(normed, ('gy', 'gz'), axis=0, tiled=True)  5.92 us
  transfers between devices with their start and end apart: 3, of which 3 were waited for; matrix products, arithmetic and copies ran while one was open for 0% of the time, Pallas kernels for 0%

commit v1 on v0

--- a/solution.py
+++ b/solution.py
@@ -1,10 +1,22 @@
+import functools
+import math
+
 import jax
 import jax.numpy as jnp
+import numpy as np
 from jax import lax
+from jax.experimental import pallas as pl
+from jax.experimental.pallas import tpu as pltpu
 from jax.sharding import PartitionSpec as P
 
 D = 18432
 DH = 256
+HALF = DH // 2
+LANES = 128
+MESH = pl.DeviceIdType.MESH
+CHUNK_HEADS = 4
+OUT_COLS = 768
+SEQS = 2
 
 
 def rotary(values, places):
@@ -85,7 +97,383 @@
     ).astype(jnp.float32)
 
 
+def layer_kernel(
+    sizes,
+    x_ref, gain_ref, freq_ref, wq_hbm, wkv_hbm, wo_hbm, kc_hbm, vc_hbm, len_ref, pos_ref,
+    out_ref,
+    wq, wkv, wo, kc, vc,
+    rows_x, stats, normed, q_send, q_recv, kv_send, kv_recv,
+    h_send, h_recv, h_spread, h_rows, total, o_send, o_recv,
+    load_sem, x_sem, stat_sem, kv_sem, q_sem, h_sem, o_sem,
+):
+    G, Y, Z = sizes
+    C = Y * Z
+    N = G * C
+    H = CHUNK_HEADS
+    chunks = wq.shape[0]
+    count = 2 * C * G
+    feats = x_ref.shape[1]
+    half_feats = feats // 2
+    out_chunks = o_send.shape[0]
+    slots = kc.shape[0] // SEQS
+    block = rows_x.shape[1] // 2
+    gx, plane = lax.axis_index("gx"), lax.axis_index("gy") * Z + lax.axis_index("gz")
+    me = gx * C + plane
+
+    def device(rank):
+        return {"gx": rank // C, "gy": rank % C // Z, "gz": rank % Z}
+
+    def load(j, source, target):
+        return pltpu.make_async_copy(source, target, load_sem.at[j])
+
+    def arrived(ref, sem):
+        pltpu.make_async_copy(ref, ref, sem).wait()
+
+    def to_all(body):
+        def step(k, carry):
+            body(lax.rem(me + k, N))
+            return carry
+
+        lax.fori_loop(1, N, step, 0)
+
+    loads = [load(0, wkv_hbm, wkv)]
+    cols = H * DH
+    for j in range(chunks):
+        loads.append(load(1 + j, wq_hbm.at[:, pl.ds(j * cols, cols)], wq.at[j]))
+    loads.append(load(1 + chunks, kc_hbm, kc))
+    loads.append(load(2 + chunks, vc_hbm, vc))
+    for j in range(chunks):
+        loads.append(load(3 + chunks + j, wo_hbm.at[pl.ds(j * cols, cols), :], wo.at[j]))
+    for j in range(1 + chunks):
+        loads[j].start()
+
+    barrier = pltpu.get_barrier_semaphore()
+
+    def greet(rank):
+        pl.semaphore_signal(barrier, inc=1, device_id=device(rank), device_id_type=MESH)
+
+    to_all(greet)
+
+    x = x_ref[...].astype(jnp.float32)
+    folded = jnp.concatenate([x[:, :half_feats], x[:, half_feats:]], 0)
+    rows_x[plane] = folded.astype(jnp.bfloat16)
+    mean = jnp.sum(x, 1, keepdims=True) / feats
+    centered = x - mean
+    spread = jnp.sum(centered * centered, 1, keepdims=True)
+    lane = lax.broadcasted_iota(jnp.int32, (block, LANES), 1)
+    stats[me] = jnp.where(lane == 0, mean, spread)
+
+    pl.semaphore_wait(barrier, N - 1)
+
+    def send_rows(k, carry):
+        rank = gx * C + lax.rem(plane + k, C)
+        pltpu.make_async_remote_copy(
+            src_ref=rows_x.at[plane], dst_ref=rows_x.at[plane],
+            send_sem=x_sem.at[0], recv_sem=x_sem.at[1],
+            device_id=device(rank), device_id_type=MESH,
+        ).start()
+        return carry
+
+    lax.fori_loop(1, C, send_rows, 0)
+
+    def send_stats(rank):
+        pltpu.make_async_remote_copy(
+            src_ref=stats.at[me], dst_ref=stats.at[me],
+            send_sem=stat_sem.at[0], recv_sem=stat_sem.at[1],
+            device_id=device(rank), device_id_type=MESH,
+        ).start()
+
+    to_all(send_stats)
+
+    row = lax.broadcasted_iota(jnp.int32, (SEQS * H, LANES), 0)
+    place = jnp.where(row < H, pos_ref[0], pos_ref[1]).astype(jnp.float32)
+    angle = place * freq_ref[...]
+    turns = jnp.floor(angle * (0.5 / math.pi) + 0.5)
+    angle = angle - turns * 6.28125
+    angle = angle - turns * (4058 / 2097152)
+    angle = angle - turns * (2 * math.pi - 6.28125 - 4058 / 2097152)
+    cosine, sine = jnp.cos(angle), jnp.sin(angle)
+
+    def turned(t, cos, sin):
+        t1, t2 = t[:, :HALF], t[:, HALF:]
+        return jnp.concatenate([t1 * cos - t2 * sin, t2 * cos + t1 * sin], 1)
+
+    cos_all = jnp.concatenate([cosine] * C, 0)
+    sin_all = jnp.concatenate([sine] * C, 0)
+
+    arrived(stats.at[pl.ds(0, N - 1)], stat_sem.at[1])
+    arrived(rows_x.at[pl.ds(0, C - 1)], x_sem.at[1])
+
+    for pair in range(C // 2):
+        lows, highs = [], []
+        for c in (2 * pair, 2 * pair + 1):
+            parts = [stats[g * C + c] for g in range(G)]
+            means = [p[:, 0:1] for p in parts]
+            mean = functools.reduce(jnp.add, means) / G
+            squares = functools.reduce(jnp.add, [p[:, 1:2] for p in parts])
+            between = functools.reduce(jnp.add, [(m - mean) * (m - mean) for m in means])
+            scale = lax.rsqrt((squares + feats * between) / (feats * G) + 1e-05)
+            folded = rows_x[c].astype(jnp.float32)
+            lows.append((folded[:block] - mean) * scale)
+            highs.append((folded[block:] - mean) * scale)
+        rows = pl.ds(2 * pair * block, 2 * block)
+        low = jnp.concatenate(lows, 0) * gain_ref[:, :half_feats]
+        high = jnp.concatenate(highs, 0) * gain_ref[:, half_feats:]
+        normed[rows, pl.ds(0, half_feats)] = low.astype(jnp.bfloat16)
+        normed[rows, pl.ds(half_feats, half_feats)] = high.astype(jnp.bfloat16)
+
+    loads[0].wait()
+    part = jnp.dot(normed[...], wkv[...], preferred_element_type=jnp.float32)
+    for h in range(H):
+        kv_send[pl.ds(h, count, stride=H), :] = part
+
+    def send_kv(rank):
+        pltpu.make_async_remote_copy(
+            src_ref=kv_send.at[pl.ds(pl.multiple_of(rank * SEQS * H, SEQS * H), SEQS * H), :],
+            dst_ref=kv_recv.at[me],
+            send_sem=kv_sem.at[0], recv_sem=kv_sem.at[1],
+            device_id=device(rank), device_id_type=MESH,
+        ).start()
+
+    to_all(send_kv)
+    own = pl.ds(pl.multiple_of(me * SEQS * H, SEQS * H), SEQS * H)
+    kv_recv[me] = kv_send[own, :]
+
+    for j in range(chunks):
+        loads[1 + j].wait()
+        if j == 0:
+            loads[1 + chunks].start()
+            loads[2 + chunks].start()
+        loads[3 + chunks + j].start()
+        for h in range(0, H, 2):
+            part = jnp.dot(
+                normed[...], wq[j, :, h * DH:(h + 2) * DH], preferred_element_type=jnp.float32
+            )
+            for i in range(2):
+                for side in range(2):
+                    at = i * DH + side * HALF
+                    q_send[j, side, pl.ds(h + i, count, stride=H), :] = part[:, at:at + HALF]
+
+        def send_query(rank):
+            rows = pl.ds(pl.multiple_of(rank * SEQS * H, SEQS * H), SEQS * H)
+            pltpu.make_async_remote_copy(
+                src_ref=q_send.at[j, :, rows, :], dst_ref=q_recv.at[j, me],
+                send_sem=q_sem.at[0, j], recv_sem=q_sem.at[1, j],
+                device_id=device(rank), device_id_type=MESH,
+            ).start()
+
+        to_all(send_query)
+        q_recv[j, me] = q_send[j, :, own, :]
+
+    arrived(kv_recv.at[pl.ds(0, N - 1)], kv_sem.at[1])
+    pieces = []
+    for c in range(C):
+        pieces.append(functools.reduce(jnp.add, [kv_recv[g * C + c] for g in range(G)]))
+    keyval = jnp.concatenate(pieces, 1).astype(jnp.bfloat16).astype(jnp.float32)
+    rot_key = turned(keyval[:, :DH], cosine, sine).astype(jnp.bfloat16).astype(jnp.float32)
+    key_all = jnp.concatenate([rot_key] * C, 0)
+    value_all = jnp.concatenate([keyval[:, DH:]] * C, 0)
+
+    loads[1 + chunks].wait()
+    loads[2 + chunks].wait()
+    rows_all = C * SEQS * H
+    row = lax.broadcasted_iota(jnp.int32, (rows_all, SEQS * slots), 0)
+    slot = lax.broadcasted_iota(jnp.int32, (rows_all, SEQS * slots), 1)
+    second = lax.rem(row, SEQS * H) >= H
+    base = jnp.where(second, slots, 0)
+    live = (slot >= base) & (slot < base + jnp.where(second, len_ref[1], len_ref[0]))
+    scale = DH ** (-0.5)
+
+    for j in range(chunks):
+        arrived(q_recv.at[j, pl.ds(0, N - 1)], q_sem.at[1, j])
+        blocks = []
+        for c in range(C):
+            sides = []
+            for side in range(2):
+                sides.append(
+                    functools.reduce(jnp.add, [q_recv[j, g * C + c, side] for g in range(G)])
+                )
+            blocks.append(jnp.concatenate(sides, 1))
+        query = jnp.concatenate(blocks, 0).astype(jnp.bfloat16).astype(jnp.float32)
+        rot_query = turned(query, cos_all, sin_all).astype(jnp.bfloat16)
+        scores = lax.dot_general(
+            rot_query, kc[...], (((1,), (1,)), ((), ())), preferred_element_type=jnp.float32
+        ) * scale
+        selfish = jnp.sum(rot_query.astype(jnp.float32) * key_all, 1, keepdims=True) * scale
+        masked = jnp.where(live, scores, -1e30)
+        peak = jnp.maximum(jnp.max(masked, 1, keepdims=True), selfish)
+        expo = jnp.where(live, jnp.exp(masked - peak), 0.0)
+        expo_self = jnp.exp(selfish - peak)
+        denominator = jnp.sum(expo, 1, keepdims=True) + expo_self
+        probs = (expo / denominator).astype(jnp.bfloat16)
+        probs_self = (expo_self / denominator).astype(jnp.bfloat16).astype(jnp.float32)
+        mixed = jnp.dot(probs, vc[...], preferred_element_type=jnp.float32)
+        mixed = mixed + probs_self * value_all
+        for c in range(C):
+            tile = mixed[c * SEQS * H:(c + 1) * SEQS * H]
+            h_send[j, c] = jnp.concatenate([tile[:, :HALF], tile[:, HALF:]], 0).astype(jnp.bfloat16)
+
+        def send_heads(rank):
+            pltpu.make_async_remote_copy(
+                src_ref=h_send.at[j, rank % C], dst_ref=h_recv.at[j, me],
+                send_sem=h_sem.at[0, j], recv_sem=h_sem.at[1, j],
+                device_id=device(rank), device_id_type=MESH,
+            ).start()
+
+        to_all(send_heads)
+        h_recv[j, me] = h_send[j, plane]
+
+    def gather_heads(j):
+        arrived(h_recv.at[j, pl.ds(0, N - 1)], h_sem.at[1, j])
+        for rank in range(N):
+            tile = h_recv[j, rank].astype(jnp.float32)
+            for side in range(2):
+                h_spread[side, rank * SEQS * H:(rank + 1) * SEQS * H] = tile[
+                    side * SEQS * H:(side + 1) * SEQS * H
+                ]
+        for h in range(H):
+            for side in range(2):
+                at = h * DH + side * HALF
+                h_rows[j, :, at:at + HALF] = h_spread[
+                    side, pl.ds(h, count, stride=H), :
+                ].astype(jnp.bfloat16)
+
+    for j in range(chunks):
+        gather_heads(j)
+        loads[3 + chunks + j].wait()
+
+        def columns(n, carry):
+            at = pl.ds(pl.multiple_of(n * OUT_COLS, OUT_COLS), OUT_COLS)
+            part = jnp.dot(h_rows[j], wo[j, :, at], preferred_element_type=jnp.float32)
+            if j > 0:
+                part = part + total[:, at]
+            if j < chunks - 1:
+                total[:, at] = part
+                return carry
+            for c in range(C):
+                tile = part[c * block:(c + 1) * block]
+                o_send[n, c] = jnp.concatenate(
+                    [tile[:, :OUT_COLS // 2], tile[:, OUT_COLS // 2:]], 0
+                ).astype(jnp.bfloat16)
+            for k in range(1, C):
+                other = lax.rem(plane + k, C)
+                pltpu.make_async_remote_copy(
+                    src_ref=o_send.at[n, other], dst_ref=o_recv.at[n, k - 1],
+                    send_sem=o_sem.at[0, n], recv_sem=o_sem.at[1, n],
+                    device_id=device(gx * C + other), device_id_type=MESH,
+                ).start()
+            return carry
+
+        lax.fori_loop(0, out_chunks, columns, 0)
+
+    def finish(n, carry):
+        arrived(o_recv.at[n], o_sem.at[1, n])
+        summed = o_send[n, plane].astype(jnp.float32)
+        for k in range(C - 1):
+            summed = summed + o_recv[n, k].astype(jnp.float32)
+        low = pl.multiple_of(n * OUT_COLS, OUT_COLS // 2)
+        high = pl.multiple_of(n * OUT_COLS + OUT_COLS // 2, OUT_COLS // 2)
+        out_ref[:, pl.ds(low, OUT_COLS // 2)] = summed[:block]
+        out_ref[:, pl.ds(high, OUT_COLS // 2)] = summed[block:]
+        return carry
+
+    lax.fori_loop(0, out_chunks, finish, 0)
+
+    arrived(rows_x.at[pl.ds(0, C - 1)], x_sem.at[0])
+    arrived(stats.at[pl.ds(0, N - 1)], stat_sem.at[0])
+    arrived(kv_recv.at[pl.ds(0, N - 1)], kv_sem.at[0])
+    for j in range(chunks):
+        arrived(q_recv.at[j, pl.ds(0, N - 1)], q_sem.at[0, j])
+        arrived(h_recv.at[j, pl.ds(0, N - 1)], h_sem.at[0, j])
+
+    def left(n, carry):
+        arrived(o_recv.at[n], o_sem.at[0, n])
+        return carry
+
+    lax.fori_loop(0, out_chunks, left, 0)
+
+
+def fused(
+    sizes, hidden_in, ln_gain, w_query, w_keyval, w_output, key_cache, value_cache, lengths, positions
+):
+    G, Y, Z = sizes
+    C = Y * Z
+    N = G * C
+    block, feats = hidden_in.shape
+    count = block * C
+    H = CHUNK_HEADS
+    chunks = w_query.shape[1] // (H * DH)
+    out_cols = w_output.shape[1]
+    out_chunks = out_cols // OUT_COLS
+    keys = key_cache.reshape(-1, DH)
+    values = value_cache.reshape(-1, DH)
+    freqs = np.exp(-np.log(10000.0) * np.arange(HALF) / HALF).astype(np.float32)[None, :]
+    bf16, f32 = jnp.bfloat16, jnp.float32
+    vmem = pl.BlockSpec(memory_space=pltpu.VMEM)
+    smem = pl.BlockSpec(memory_space=pltpu.SMEM)
+    anywhere = pl.BlockSpec(memory_space=pl.ANY)
+    tile = SEQS * H
+    return pl.pallas_call(
+        functools.partial(layer_kernel, sizes),
+        out_shape=jax.ShapeDtypeStruct((block, out_cols), f32),
+        in_specs=[vmem, vmem, vmem] + [anywhere] * 5 + [smem, smem],
+        out_specs=vmem,
+        scratch_shapes=[
+            pltpu.VMEM((chunks, feats, H * DH), bf16),
+            pltpu.VMEM(w_keyval.shape, bf16),
+            pltpu.VMEM((chunks, H * DH, out_cols), bf16),
+            pltpu.VMEM(keys.shape, bf16),
+            pltpu.VMEM(values.shape, bf16),
+            pltpu.VMEM((C, 2 * block, feats // 2), bf16),
+            pltpu.VMEM((N, block, LANES), f32),
+            pltpu.VMEM((count, feats), bf16),
+            pltpu.VMEM((chunks, 2, N * tile, HALF), f32),
+            pltpu.VMEM((chunks, N, 2, tile, HALF), f32),
+            pltpu.VMEM((N * tile, w_keyval.shape[1]), f32),
+            pltpu.VMEM((N, tile, w_keyval.shape[1]), f32),
+            pltpu.VMEM((chunks, C, 2 * tile, HALF), bf16),
+            pltpu.VMEM((chunks, N, 2 * tile, HALF), bf16),
+            pltpu.VMEM((2, N * tile, HALF), f32),
+            pltpu.VMEM((chunks, count, H * DH), bf16),
+            pltpu.VMEM((count, out_cols), f32),
+            pltpu.VMEM((out_chunks, C, 2 * block, OUT_COLS // 2), bf16),
+            pltpu.VMEM((out_chunks, C - 1, 2 * block, OUT_COLS // 2), bf16),
+            pltpu.SemaphoreType.DMA((3 + 2 * chunks,)),
+            pltpu.SemaphoreType.DMA((2,)),
+            pltpu.SemaphoreType.DMA((2,)),
+            pltpu.SemaphoreType.DMA((2,)),
+            pltpu.SemaphoreType.DMA((2, chunks)),
+            pltpu.SemaphoreType.DMA((2, chunks)),
+            pltpu.SemaphoreType.DMA((2, out_chunks)),
+        ],
+        compiler_params=pltpu.CompilerParams(
+            collective_id=0, has_side_effects=True, vmem_limit_bytes=62 * 1024 * 1024
+        ),
+    )(
+        hidden_in, ln_gain.reshape(1, -1), jnp.asarray(freqs), w_query, w_keyval, w_output,
+        keys, values, lengths, positions,
+    )
+
+
 def solution(mesh):
+    sizes = (mesh.shape["gx"], mesh.shape["gy"], mesh.shape["gz"])
+    plane = sizes[1] * sizes[2]
+
+    def layer(*args):
+        hidden_in, _, w_query, w_keyval, w_output, key_cache = args[:6]
+        fits = (
+            key_cache.shape[0] == SEQS
+            and hidden_in.shape[0] == 8
+            and plane % 2 == 0
+            and hidden_in.shape[1] % (2 * LANES) == 0
+            and w_query.shape[1] % (CHUNK_HEADS * DH) == 0
+            and w_keyval.shape[1] == LANES
+            and w_output.shape[1] % OUT_COLS == 0
+        )
+        if fits:
+            return fused(sizes, *args)
+        return per_device(*args)
+
     in_specs = (
         P(("grp", "gy", "gz"), "gx"),
         P("gx"),
@@ -98,6 +486,4 @@
         P(("grp", "gx", "gy", "gz")),
     )
     out_specs = P(("grp", "gy", "gz"), "gx")
-    return jax.shard_map(
-        per_device, mesh=mesh, in_specs=in_specs, out_specs=out_specs, check_vma=False
-    )
+    return jax.shard_map(layer, mesh=mesh, in_specs=in_specs, out_specs=out_specs, check_vma=False)

time: 141 us -> 41.3 us (0.29)
  blocking collectives: 64.5 us -> 0 us
  Pallas kernels: 0 us -> 38.1 us
  matrix products: 24.9 us -> 0 us
  waiting for transfers between devices: 24.5 us -> 0 us
  between operations: 14.3 us -> 0.01 us
  starting transfers between devices: 6.48 us -> 0 us
  other arithmetic: 4.27 us -> 0 us
    pallas_call x0 -> x1, Pallas kernels: none -> 38.1 us  [fused(): pl.pallas_call(functools.partial(layer_kernel, sizes), out_shape=jax.Shap...]
    dot_general x6 -> x0, matrix products: 24.9 us -> none  [the longest x1 12.3 us: per_device(): jnp.dot(lax.all_gather(head_block, 'gx', axis=0, tiled=True), w_output, p...]
    unnamed x1 -> x0, blocking collectives: 24.8 us -> none
    all_gather x2 -> x0, blocking collectives: 19.8 us -> none  [the longest x1 13.9 us: per_device(): lax.all_gather(head_block, 'gx', axis=0, tiled=True)]
    reduce_scatter x1 -> x0, waiting for transfers between devices: 17.8 us -> none  [per_device(): lax.psum_scatter(partials.astype(jnp.bfloat16), ('gy', 'gz'), scatter_dim...]
    psum x1 -> x0, blocking collectives: 13.5 us -> none  [per_device(): totals, squares = lax.psum((jnp.sum(xf, 1), jnp.sum(xf * xf, 1)), 'gx')]
    all_to_all x2 -> x0, waiting for transfers between devices: 6.75 us -> none  [the longest x1 3.81 us: per_device(): lax.all_to_all(query_part, ('gy', 'gz'), split_axis=0, concat_axis=1, til...]
    all_to_all x2 -> x0, starting transfers between devices: 6.44 us -> none  [the longest x1 3.27 us: per_device(): lax.all_to_all(query_part, ('gy', 'gz'), split_axis=0, concat_axis=1, til...]
  transfers between devices with their start and end apart: 3 -> 0, of which waited for: 3 -> 0; matrix products, arithmetic and copies ran while one was open for 0% -> 0% of each run, Pallas kernels for 0% -> 0%
where the time goes in v1:
time: 41.3 us; the launch traced here: 41.1 us
  Pallas kernels  38.1 us (92%)
  local copies, waits for them, and re-layouts  2.93 us (7%)
    pallas_call x1, Pallas kernels, fused(): pl.pallas_call(functools.partial(layer_kernel, sizes), out_shape=jax.Shap...  38.1 us
    unnamed x1, local copies, waits for them, and re-layouts  1.58 us
    reshape x1, local copies, waits for them, and re-layouts, fused(): ln_gain.reshape(1, -1)  1.35 us

profile of v1, /device:TPU:0, one launch (start us, length us, event | category | flops | bytes accessed | tf_op | source)
XLA Modules:
  0.0 41.1 jit_solution(9670592124114270452)
XLA Ops:
  0.0 1.3 %reshape.9.gain_ref = f32[1,4608]{1,0:T(1,128)} reshape(f32[4608]{0:T(1024)} %param.11) | data formatting | bytes 36864 | tf_op jit(solution)/shard_map/reshape | solution.py:453
  1.3 38.1 %shard_map.100 = f32[8,4608]{1,0:T(8,128)} custom-call(bf16[8,4608]{1,0:T(8,128)(2,1)} %x_ref.1, f32[1,4608]{1,0:T(1,128)} %reshape.9.gain_ref, f32[1,128]{1,0:T(1,128)} %constant.2.clone.freq_ref, bf16[4608,3072]{1,0:T(8,128)(2,1)} %wq_hbm.1, bf16[4608,128]{1,0:T(8,128)(2,1)} %wkv_hbm.1, bf16[3072,4608]{1,0:T(8,128)(2,1)} %wo_hbm.1, ...), custom_call_target="tpu_custom_call" | custom-call | tf_op jit(solution)/shard_map/pallas_call | solution.py:416
  39.5 1.6 %copy.12 = f32[8,4608]{1,0:T(8,128)} copy(f32[8,4608]{1,0:T(8,128)} %shard_map.100) | data formatting | bytes 294912

commit v2 on v1

--- a/solution.py
+++ b/solution.py
@@ -99,12 +99,13 @@
 
 def layer_kernel(
     sizes,
-    x_ref, gain_ref, freq_ref, wq_hbm, wkv_hbm, wo_hbm, kc_hbm, vc_hbm, len_ref, pos_ref,
+    x_hbm, gain_hbm, freq_hbm, wq_hbm, wkv_hbm, wo_hbm, kc_hbm, vc_hbm, len_hbm, pos_hbm,
     out_ref,
+    x_ref, gain_ref, freq_ref, len_ref, pos_ref,
     wq, wkv, wo, kc, vc,
     rows_x, stats, normed, q_send, q_recv, kv_send, kv_recv,
-    h_send, h_recv, h_spread, h_rows, total, o_send, o_recv,
-    load_sem, x_sem, stat_sem, kv_sem, q_sem, h_sem, o_sem,
+    h_send, h_recv, spread, h_rows, total, o_send, o_recv,
+    small_sem, load_sem, x_sem, stat_sem, kv_sem, q_sem, h_sem, o_sem,
 ):
     G, Y, Z = sizes
     C = Y * Z
@@ -114,10 +115,12 @@
     count = 2 * C * G
     feats = x_ref.shape[1]
     half_feats = feats // 2
+    quarter = feats // 4
     out_chunks = o_send.shape[0]
     slots = kc.shape[0] // SEQS
-    block = rows_x.shape[1] // 2
-    gx, plane = lax.axis_index("gx"), lax.axis_index("gy") * Z + lax.axis_index("gz")
+    block = x_ref.shape[0]
+    gx, gy, gz = (lax.axis_index(axis) for axis in ("gx", "gy", "gz"))
+    plane = gy * Z + gz
     me = gx * C + plane
 
     def device(rank):
@@ -136,6 +139,22 @@
 
         lax.fori_loop(1, N, step, 0)
 
+    barrier = pltpu.get_barrier_semaphore()
+
+    def greet(rank):
+        pl.semaphore_signal(barrier, inc=1, device_id=device(rank), device_id_type=MESH)
+
+    to_all(greet)
+
+    smalls = [
+        pltpu.make_async_copy(source, target, small_sem.at[i])
+        for i, (source, target) in enumerate(
+            [(x_hbm, x_ref), (gain_hbm, gain_ref), (freq_hbm, freq_ref),
+             (len_hbm, len_ref), (pos_hbm, pos_ref)]
+        )
+    ]
+    for copy in smalls:
+        copy.start()
     loads = [load(0, wkv_hbm, wkv)]
     cols = H * DH
     for j in range(chunks):
@@ -147,34 +166,29 @@
     for j in range(1 + chunks):
         loads[j].start()
 
-    barrier = pltpu.get_barrier_semaphore()
-
-    def greet(rank):
-        pl.semaphore_signal(barrier, inc=1, device_id=device(rank), device_id_type=MESH)
-
-    to_all(greet)
-
+    smalls[0].wait()
     x = x_ref[...].astype(jnp.float32)
-    folded = jnp.concatenate([x[:, :half_feats], x[:, half_feats:]], 0)
-    rows_x[plane] = folded.astype(jnp.bfloat16)
+    for half in range(2):
+        at = half * half_feats
+        folded = jnp.concatenate([x[:, at:at + quarter], x[:, at + quarter:at + half_feats]], 0)
+        rows_x[half, plane] = folded.astype(jnp.bfloat16)
     mean = jnp.sum(x, 1, keepdims=True) / feats
     centered = x - mean
-    spread = jnp.sum(centered * centered, 1, keepdims=True)
+    squares = jnp.sum(centered * centered, 1, keepdims=True)
     lane = lax.broadcasted_iota(jnp.int32, (block, LANES), 1)
-    stats[me] = jnp.where(lane == 0, mean, spread)
+    stats[me] = jnp.where(lane == 0, mean, squares)
 
     pl.semaphore_wait(barrier, N - 1)
 
-    def send_rows(k, carry):
-        rank = gx * C + lax.rem(plane + k, C)
-        pltpu.make_async_remote_copy(
-            src_ref=rows_x.at[plane], dst_ref=rows_x.at[plane],
-            send_sem=x_sem.at[0], recv_sem=x_sem.at[1],
-            device_id=device(rank), device_id_type=MESH,
-        ).start()
-        return carry
-
-    lax.fori_loop(1, C, send_rows, 0)
+    def send_rows(half):
+        for k in range(1, C):
+            pltpu.make_async_remote_copy(
+                src_ref=rows_x.at[half, plane], dst_ref=rows_x.at[half, plane],
+                send_sem=x_sem.at[0, half], recv_sem=x_sem.at[1, half],
+                device_id=device(gx * C + lax.rem(plane + k, C)), device_id_type=MESH,
+            ).start()
+
+    send_rows(0)
 
     def send_stats(rank):
         pltpu.make_async_remote_copy(
@@ -184,6 +198,10 @@
         ).start()
 
     to_all(send_stats)
+    send_rows(1)
+
+    for copy in smalls[1:]:
+        copy.wait()
 
     row = lax.broadcasted_iota(jnp.int32, (SEQS * H, LANES), 0)
     place = jnp.where(row < H, pos_ref[0], pos_ref[1]).astype(jnp.float32)
@@ -202,74 +220,95 @@
     sin_all = jnp.concatenate([sine] * C, 0)
 
     arrived(stats.at[pl.ds(0, N - 1)], stat_sem.at[1])
-    arrived(rows_x.at[pl.ds(0, C - 1)], x_sem.at[1])
-
-    for pair in range(C // 2):
-        lows, highs = [], []
-        for c in (2 * pair, 2 * pair + 1):
-            parts = [stats[g * C + c] for g in range(G)]
-            means = [p[:, 0:1] for p in parts]
-            mean = functools.reduce(jnp.add, means) / G
-            squares = functools.reduce(jnp.add, [p[:, 1:2] for p in parts])
-            between = functools.reduce(jnp.add, [(m - mean) * (m - mean) for m in means])
-            scale = lax.rsqrt((squares + feats * between) / (feats * G) + 1e-05)
-            folded = rows_x[c].astype(jnp.float32)
-            lows.append((folded[:block] - mean) * scale)
-            highs.append((folded[block:] - mean) * scale)
-        rows = pl.ds(2 * pair * block, 2 * block)
-        low = jnp.concatenate(lows, 0) * gain_ref[:, :half_feats]
-        high = jnp.concatenate(highs, 0) * gain_ref[:, half_feats:]
-        normed[rows, pl.ds(0, half_feats)] = low.astype(jnp.bfloat16)
-        normed[rows, pl.ds(half_feats, half_feats)] = high.astype(jnp.bfloat16)
+    moments = []
+    for c in range(C):
+        parts = [stats[g * C + c] for g in range(G)]
+        means = [p[:, 0:1] for p in parts]
+        mean = functools.reduce(jnp.add, means) / G
+        squares = functools.reduce(jnp.add, [p[:, 1:2] for p in parts])
+        between = functools.reduce(jnp.add, [(m - mean) * (m - mean) for m in means])
+        moments.append((mean, lax.rsqrt((squares + feats * between) / (feats * G) + 1e-05)))
+
+    def normalize(half):
+        arrived(rows_x.at[half, pl.ds(0, C - 1)], x_sem.at[1, half])
+        for pair in range(C // 2):
+            lows, highs = [], []
+            for c in (2 * pair, 2 * pair + 1):
+                mean, scale = moments[c]
+                folded = rows_x[half, c].astype(jnp.float32)
+                lows.append((folded[:block] - mean) * scale)
+                highs.append((folded[block:] - mean) * scale)
+            rows = pl.ds(2 * pair * block, 2 * block)
+            for at, part in ((half * half_feats, lows), (half * half_feats + quarter, highs)):
+                part = jnp.concatenate(part, 0) * gain_ref[pl.ds(at, quarter)][None, :]
+                normed[rows, pl.ds(at, quarter)] = part.astype(jnp.bfloat16)
+
+    normalize(0)
+    loads[1].wait()
+    for h in range(0, H, 2):
+        at = slice(h * DH, (h + 2) * DH)
+        total[:, at] = jnp.dot(
+            normed[:, :half_feats], wq[0, :half_feats, at], preferred_element_type=jnp.float32
+        )
+    normalize(1)
 
     loads[0].wait()
     part = jnp.dot(normed[...], wkv[...], preferred_element_type=jnp.float32)
-    for h in range(H):
-        kv_send[pl.ds(h, count, stride=H), :] = part
+    for rank in range(N):
+        kv_send[rank] = part[rank * SEQS:(rank + 1) * SEQS]
 
     def send_kv(rank):
         pltpu.make_async_remote_copy(
-            src_ref=kv_send.at[pl.ds(pl.multiple_of(rank * SEQS * H, SEQS * H), SEQS * H), :],
-            dst_ref=kv_recv.at[me],
+            src_ref=kv_send.at[rank], dst_ref=kv_recv.at[me],
             send_sem=kv_sem.at[0], recv_sem=kv_sem.at[1],
             device_id=device(rank), device_id_type=MESH,
         ).start()
 
     to_all(send_kv)
-    own = pl.ds(pl.multiple_of(me * SEQS * H, SEQS * H), SEQS * H)
-    kv_recv[me] = kv_send[own, :]
+    kv_recv[me] = kv_send[me]
 
     for j in range(chunks):
-        loads[1 + j].wait()
+        if j > 0:
+            loads[1 + j].wait()
         if j == 0:
             loads[1 + chunks].start()
             loads[2 + chunks].start()
         loads[3 + chunks + j].start()
         for h in range(0, H, 2):
-            part = jnp.dot(
-                normed[...], wq[j, :, h * DH:(h + 2) * DH], preferred_element_type=jnp.float32
-            )
+            at = slice(h * DH, (h + 2) * DH)
+            if j == 0:
+                part = total[:, at] + jnp.dot(
+                    normed[:, half_feats:], wq[j, half_feats:, at],
+                    preferred_element_type=jnp.float32,
+                )
+            else:
+                part = jnp.dot(normed[...], wq[j, :, at], preferred_element_type=jnp.float32)
             for i in range(2):
                 for side in range(2):
                     at = i * DH + side * HALF
-                    q_send[j, side, pl.ds(h + i, count, stride=H), :] = part[:, at:at + HALF]
+                    spread[side, pl.ds(h + i, count, stride=H), :] = part[:, at:at + HALF]
+        tiles = [spread[side].reshape(N, SEQS * H, HALF) for side in range(2)]
+        q_send[j] = jnp.concatenate(tiles, 1)
 
         def send_query(rank):
-            rows = pl.ds(pl.multiple_of(rank * SEQS * H, SEQS * H), SEQS * H)
             pltpu.make_async_remote_copy(
-                src_ref=q_send.at[j, :, rows, :], dst_ref=q_recv.at[j, me],
+                src_ref=q_send.at[j, rank], dst_ref=q_recv.at[j, me],
                 send_sem=q_sem.at[0, j], recv_sem=q_sem.at[1, j],
                 device_id=device(rank), device_id_type=MESH,
             ).start()
 
         to_all(send_query)
-        q_recv[j, me] = q_send[j, :, own, :]
+        q_recv[j, me] = q_send[j, me]
 
     arrived(kv_recv.at[pl.ds(0, N - 1)], kv_sem.at[1])
     pieces = []
     for c in range(C):
         pieces.append(functools.reduce(jnp.add, [kv_recv[g * C + c] for g in range(G)]))
-    keyval = jnp.concatenate(pieces, 1).astype(jnp.bfloat16).astype(jnp.float32)
+    keyval = jnp.concatenate(pieces, 1)
+    keyval = jnp.concatenate(
+        [jnp.broadcast_to(keyval[i:i + 1], (H, 2 * DH)) for i in range(SEQS)], 0
+    )
+    keyval = keyval.astype(jnp.bfloat16).astype(jnp.float32)
     rot_key = turned(keyval[:, :DH], cosine, sine).astype(jnp.bfloat16).astype(jnp.float32)
     key_all = jnp.concatenate([rot_key] * C, 0)
     value_all = jnp.concatenate([keyval[:, DH:]] * C, 0)
@@ -288,12 +327,8 @@
         arrived(q_recv.at[j, pl.ds(0, N - 1)], q_sem.at[1, j])
         blocks = []
         for c in range(C):
-            sides = []
-            for side in range(2):
-                sides.append(
-                    functools.reduce(jnp.add, [q_recv[j, g * C + c, side] for g in range(G)])
-                )
-            blocks.append(jnp.concatenate(sides, 1))
+            tile = functools.reduce(jnp.add, [q_recv[j, g * C + c] for g in range(G)])
+            blocks.append(jnp.concatenate([tile[:SEQS * H], tile[SEQS * H:]], 1))
         query = jnp.concatenate(blocks, 0).astype(jnp.bfloat16).astype(jnp.float32)
         rot_query = turned(query, cos_all, sin_all).astype(jnp.bfloat16)
         scores = lax.dot_general(
@@ -328,13 +363,13 @@
         for rank in range(N):
             tile = h_recv[j, rank].astype(jnp.float32)
             for side in range(2):
-                h_spread[side, rank * SEQS * H:(rank + 1) * SEQS * H] = tile[
+                spread[side, rank * SEQS * H:(rank + 1) * SEQS * H] = tile[
                     side * SEQS * H:(side + 1) * SEQS * H
                 ]
         for h in range(H):
             for side in range(2):
                 at = h * DH + side * HALF
-                h_rows[j, :, at:at + HALF] = h_spread[
+                h_rows[j, :, at:at + HALF] = spread[
                     side, pl.ds(h, count, stride=H), :
                 ].astype(jnp.bfloat16)
 
@@ -379,7 +414,8 @@
 
     lax.fori_loop(0, out_chunks, finish, 0)
 
-    arrived(rows_x.at[pl.ds(0, C - 1)], x_sem.at[0])
+    for half in range(2):
+        arrived(rows_x.at[half, pl.ds(0, C - 1)], x_sem.at[0, half])
     arrived(stats.at[pl.ds(0, N - 1)], stat_sem.at[0])
     arrived(kv_recv.at[pl.ds(0, N - 1)], kv_sem.at[0])
     for j in range(chunks):
@@ -410,27 +446,31 @@
     freqs = np.exp(-np.log(10000.0) * np.arange(HALF) / HALF).astype(np.float32)[None, :]
     bf16, f32 = jnp.bfloat16, jnp.float32
     vmem = pl.BlockSpec(memory_space=pltpu.VMEM)
-    smem = pl.BlockSpec(memory_space=pltpu.SMEM)
     anywhere = pl.BlockSpec(memory_space=pl.ANY)
     tile = SEQS * H
     return pl.pallas_call(
         functools.partial(layer_kernel, sizes),
-        out_shape=jax.ShapeDtypeStruct((block, out_cols), f32),
-        in_specs=[vmem, vmem, vmem] + [anywhere] * 5 + [smem, smem],
+        out_shape=pltpu.VMEM((block, out_cols), f32),
+        in_specs=[anywhere] * 10,
         out_specs=vmem,
         scratch_shapes=[
+            pltpu.VMEM(hidden_in.shape, bf16),
+            pltpu.VMEM(ln_gain.shape, f32),
+            pltpu.VMEM(freqs.shape, f32),
+            pltpu.SMEM(lengths.shape, jnp.int32),
+            pltpu.SMEM(positions.shape, jnp.int32),
             pltpu.VMEM((chunks, feats, H * DH), bf16),
             pltpu.VMEM(w_keyval.shape, bf16),
             pltpu.VMEM((chunks, H * DH, out_cols), bf16),
             pltpu.VMEM(keys.shape, bf16),
             pltpu.VMEM(values.shape, bf16),
-            pltpu.VMEM((C, 2 * block, feats // 2), bf16),
+            pltpu.VMEM((2, C, 2 * block, feats // 4), bf16),
             pltpu.VMEM((N, block, LANES), f32),
             pltpu.VMEM((count, feats), bf16),
-            pltpu.VMEM((chunks, 2, N * tile, HALF), f32),
-            pltpu.VMEM((chunks, N, 2, tile, HALF), f32),
-            pltpu.VMEM((N * tile, w_keyval.shape[1]), f32),
-            pltpu.VMEM((N, tile, w_keyval.shape[1]), f32),
+            pltpu.VMEM((chunks, N, 2 * tile, HALF), f32),
+            pltpu.VMEM((chunks, N, 2 * tile, HALF), f32),
+            pltpu.VMEM((N, SEQS, w_keyval.shape[1]), f32),
+            pltpu.VMEM((N, SEQS, w_keyval.shape[1]), f32),
             pltpu.VMEM((chunks, C, 2 * tile, HALF), bf16),
             pltpu.VMEM((chunks, N, 2 * tile, HALF), bf16),
             pltpu.VMEM((2, N * tile, HALF), f32),
@@ -438,8 +478,9 @@
             pltpu.VMEM((count, out_cols), f32),
             pltpu.VMEM((out_chunks, C, 2 * block, OUT_COLS // 2), bf16),
             pltpu.VMEM((out_chunks, C - 1, 2 * block, OUT_COLS // 2), bf16),
+            pltpu.SemaphoreType.DMA((5,)),
             pltpu.SemaphoreType.DMA((3 + 2 * chunks,)),
-            pltpu.SemaphoreType.DMA((2,)),
+            pltpu.SemaphoreType.DMA((2, 2)),
             pltpu.SemaphoreType.DMA((2,)),
             pltpu.SemaphoreType.DMA((2,)),
             pltpu.SemaphoreType.DMA((2, chunks)),
@@ -450,22 +491,22 @@
             collective_id=0, has_side_effects=True, vmem_limit_bytes=62 * 1024 * 1024
         ),
     )(
-        hidden_in, ln_gain.reshape(1, -1), jnp.asarray(freqs), w_query, w_keyval, w_output,
+        hidden_in, ln_gain, jnp.asarray(freqs), w_query, w_keyval, w_output,
         keys, values, lengths, positions,
     )
 
 
 def solution(mesh):
     sizes = (mesh.shape["gx"], mesh.shape["gy"], mesh.shape["gz"])
-    plane = sizes[1] * sizes[2]
 
     def layer(*args):
         hidden_in, _, w_query, w_keyval, w_output, key_cache = args[:6]
         fits = (
             key_cache.shape[0] == SEQS
             and hidden_in.shape[0] == 8
-            and plane % 2 == 0
-            and hidden_in.shape[1] % (2 * LANES) == 0
+            and sizes[1] * sizes[2] % 2 == 0
+            and w_keyval.shape[1] * sizes[1] * sizes[2] == 2 * DH
+            and hidden_in.shape[1] % (4 * LANES) == 0
             and w_query.shape[1] % (CHUNK_HEADS * DH) == 0
             and w_keyval.shape[1] == LANES
             and w_output.shape[1] % OUT_COLS == 0

time: 41.3 us -> 36.7 us (0.89)
  local copies, waits for them, and re-layouts: 2.93 us -> 0.66 us
  Pallas kernels: 38.1 us -> 35.9 us
    pallas_call x1, Pallas kernels: 38.1 us -> 35.9 us  [fused(): pl.pallas_call(functools.partial(layer_kernel, sizes), out_shape=pltpu.VM...]
    reshape x1 -> x0, local copies, waits for them, and re-layouts: 1.35 us -> none  [fused(): ln_gain.reshape(1, -1)]
    unnamed x1, local copies, waits for them, and re-layouts: 1.58 us -> 0.66 us
where the time goes in v2:
time: 36.7 us; the launch traced here: 36.6 us
  Pallas kernels  35.9 us (98%)
  local copies, waits for them, and re-layouts  0.66 us (2%)
    pallas_call x1, Pallas kernels, fused(): pl.pallas_call(functools.partial(layer_kernel, sizes), out_shape=pltpu.VM...  35.9 us

profile of v2, /device:TPU:0, one launch (start us, length us, event | category | flops | bytes accessed | tf_op | source)
XLA Modules:
  0.0 36.6 jit_solution(3198000415927662898)
XLA Ops:
  0.0 35.9 %shard_map.100 = f32[8,4608]{1,0:T(8,128)S(1)} custom-call(bf16[8,4608]{1,0:T(8,128)(2,1)} %x_hbm.1, f32[4608]{0:T(1024)} %gain_hbm.1, f32[1,128]{1,0:T(1,128)} %constant.2.clone.freq_hbm, bf16[4608,3072]{1,0:T(8,128)(2,1)} %wq_hbm.1, bf16[4608,128]{1,0:T(8,128)(2,1)} %wkv_hbm.1, bf16[3072,4608]{1,0:T(8,128)(2,1)} %wo_hbm.1, bf16[1024,256]{1,0:T(8,128)(2,1)} %bitcast.2, ...), custom_call_target="tpu_custom_call" | custom-call | tf_op jit(solution)/shard_map/pallas_call | solution.py:451
  35.9 0.7 %copy.12 = f32[8,4608]{1,0:T(8,128)} copy(f32[8,4608]{1,0:T(8,128)S(1)} %shard_map.100) | data formatting | bytes 294912

commit v3 on v2

--- a/solution.py
+++ b/solution.py
@@ -15,7 +15,7 @@
 LANES = 128
 MESH = pl.DeviceIdType.MESH
 CHUNK_HEADS = 4
-OUT_COLS = 768
+OUT_COLS = 1536
 SEQS = 2
 
 

time: 36.7 us -> 36.5 us (level)
  no operation moved by 1% of the time
where the time goes in v3:
time: 36.5 us; the launch traced here: 36.3 us
  Pallas kernels  35.6 us (98%)
  local copies, waits for them, and re-layouts  0.66 us (2%)
    pallas_call x1, Pallas kernels, fused(): pl.pallas_call(functools.partial(layer_kernel, sizes), out_shape=pltpu.VM...  35.6 us

profile of v3, /device:TPU:0, one launch (start us, length us, event | category | flops | bytes accessed | tf_op | source)
XLA Modules:
  0.0 36.3 jit_solution(17255851579301879102)
XLA Ops:
  0.0 35.6 %shard_map.100 = f32[8,4608]{1,0:T(8,128)S(1)} custom-call(bf16[8,4608]{1,0:T(8,128)(2,1)} %x_hbm.1, f32[4608]{0:T(1024)} %gain_hbm.1, f32[1,128]{1,0:T(1,128)} %constant.2.clone.freq_hbm, bf16[4608,3072]{1,0:T(8,128)(2,1)} %wq_hbm.1, bf16[4608,128]{1,0:T(8,128)(2,1)} %wkv_hbm.1, bf16[3072,4608]{1,0:T(8,128)(2,1)} %wo_hbm.1, bf16[1024,256]{1,0:T(8,128)(2,1)} %bitcast.2, ...), custom_call_target="tpu_custom_call" | custom-call | tf_op jit(solution)/shard_map/pallas_call | solution.py:451
  35.6 0.7 %copy.12 = f32[8,4608]{1,0:T(8,128)} copy(f32[8,4608]{1,0:T(8,128)S(1)} %shard_map.100) | data formatting | bytes 294912

commit v4 on v3

--- a/solution.py
+++ b/solution.py
@@ -252,21 +252,6 @@
         )
     normalize(1)
 
-    loads[0].wait()
-    part = jnp.dot(normed[...], wkv[...], preferred_element_type=jnp.float32)
-    for rank in range(N):
-        kv_send[rank] = part[rank * SEQS:(rank + 1) * SEQS]
-
-    def send_kv(rank):
-        pltpu.make_async_remote_copy(
-            src_ref=kv_send.at[rank], dst_ref=kv_recv.at[me],
-            send_sem=kv_sem.at[0], recv_sem=kv_sem.at[1],
-            device_id=device(rank), device_id_type=MESH,
-        ).start()
-
-    to_all(send_kv)
-    kv_recv[me] = kv_send[me]
-
     for j in range(chunks):
         if j > 0:
             loads[1 + j].wait()
@@ -299,6 +284,21 @@
 
         to_all(send_query)
         q_recv[j, me] = q_send[j, me]
+        if j == 0:
+            loads[0].wait()
+            part = jnp.dot(normed[...], wkv[...], preferred_element_type=jnp.float32)
+            for rank in range(N):
+                kv_send[rank] = part[rank * SEQS:(rank + 1) * SEQS]
+
+            def send_kv(rank):
+                pltpu.make_async_remote_copy(
+                    src_ref=kv_send.at[rank], dst_ref=kv_recv.at[me],
+                    send_sem=kv_sem.at[0], recv_sem=kv_sem.at[1],
+                    device_id=device(rank), device_id_type=MESH,
+                ).start()
+
+            to_all(send_kv)
+            kv_recv[me] = kv_send[me]
 
     arrived(kv_recv.at[pl.ds(0, N - 1)], kv_sem.at[1])
     pieces = []

time: 36.5 us -> 36.1 us (0.989)
  Pallas kernels: 35.6 us -> 35.2 us
    pallas_call x1, Pallas kernels: 35.6 us -> 35.2 us  [fused(): pl.pallas_call(functools.partial(layer_kernel, sizes), out_shape=pltpu.VM...]
where the time goes in v4:
time: 36.1 us; the launch traced here: 35.9 us
  Pallas kernels  35.2 us (98%)
  local copies, waits for them, and re-layouts  0.66 us (2%)
    pallas_call x1, Pallas kernels, fused(): pl.pallas_call(functools.partial(layer_kernel, sizes), out_shape=pltpu.VM...  35.2 us

profile of v4, /device:TPU:0, one launch (start us, length us, event | category | flops | bytes accessed | tf_op | source)
XLA Modules:
  0.0 35.9 jit_solution(6037818729879477561)
XLA Ops:
  0.0 35.2 %shard_map.100 = f32[8,4608]{1,0:T(8,128)S(1)} custom-call(bf16[8,4608]{1,0:T(8,128)(2,1)} %x_hbm.1, f32[4608]{0:T(1024)} %gain_hbm.1, f32[1,128]{1,0:T(1,128)} %constant.2.clone.freq_hbm, bf16[4608,3072]{1,0:T(8,128)(2,1)} %wq_hbm.1, bf16[4608,128]{1,0:T(8,128)(2,1)} %wkv_hbm.1, bf16[3072,4608]{1,0:T(8,128)(2,1)} %wo_hbm.1, bf16[1024,256]{1,0:T(8,128)(2,1)} %bitcast.2, ...), custom_call_target="tpu_custom_call" | custom-call | tf_op jit(solution)/shard_map/pallas_call | solution.py:451
  35.3 0.7 %copy.12 = f32[8,4608]{1,0:T(8,128)} copy(f32[8,4608]{1,0:T(8,128)S(1)} %shard_map.100) | data formatting | bytes 294912
